TPU v7x, 512 devices: a whole 4x4x16 slice. The times are simulated.
512 devices in a mesh: ctx: 32 (over x, y, core), head: 16 (over z).
Axes of the slice: x: 4, y: 4, z: 16, core: 2. Of those that a mesh axis runs over, the one named last changes fastest.
Arguments:
- queries: bfloat16 [65536, 2048], P(('ctx', 'head')), may hold values from -6 to 6
- keys_base: bfloat16 [65536, 2048], P(('ctx', 'head')), may hold values from -6 to 6
- values_base: bfloat16 [65536, 2048], P(('ctx', 'head')), may hold values from -6 to 6
- grad_out: bfloat16 [65536, 2048], P(('ctx', 'head')), may hold values from -6 to 6
- key_dir: float32 [2048], replicated, may hold values from -3 to 3
- value_dir: float32 [2048], replicated, may hold values from -6 to 6
- rewards: int32 [65536], P(('ctx', 'head')), may hold values from -1000 to 1000
- episode_end: int32 [65536], P(('ctx', 'head')), may hold values 0 or 1
Outputs:
- attended: bfloat16 [65536, 2048], P(('ctx', 'head'))
- grad_queries: bfloat16 [65536, 2048], P(('ctx', 'head'))
- grad_keys: bfloat16 [65536, 2048], P(('ctx', 'head'))
- grad_values: bfloat16 [65536, 2048], P(('ctx', 'head'))
All inputs are finite; a program needn't handle non-finite values. No bound on the sum of `episode_end` on one device may be relied on, other than what follows from the above.
Results may differ from a plain program's by a relative error of at most 0.023.
Values may be sent and summed in bfloat16 or wider, within the bound.
A program may use at most 64 MiB of HBM per device.

v0:
```python
import functools
import math

import jax
import jax.numpy as jnp
from jax import lax
from jax.experimental import pallas as pl
from jax.experimental.pallas import tpu as pltpu
from jax.sharding import PartitionSpec as P

HEAD_DIM = 128
BF16 = jnp.bfloat16
F32 = jnp.float32
MESH = pl.DeviceIdType.MESH
K, V, Q, G = range(4)
O, DQ, DK, DV = range(4)
UP, DOWN = range(2)


def dot_nt(a, b):
    return lax.dot_general(a, b, (((1,), (1,)), ((), ())), preferred_element_type=F32)


def dot_tn(a, b):
    return lax.dot_general(a, b, (((0,), (0,)), ((), ())), preferred_element_type=F32)


def layer(
    n_ctx, n_head, rows, all_rows,
    q_hbm, k_hbm, v_hbm, g_hbm, kdir_ref, vdir_ref, rew_ref, end_ref,
    o_hbm, dq_hbm, dk_hbm, dv_hbm,
    send_in, in_up, in_down, send_out, out_up, out_down,
    kbuf, vbuf, dk_acc, dv_acc, q_in, g_in, grad_send, grad_recv,
    small, suffix, ctx_val, ctx_got,
    load_sem, store_sem, ring_ssem, ring_rsem, halo_ssem, halo_rsem, small_ssem, small_rsem,
):
    c = lax.axis_index("ctx")
    h = lax.axis_index("head")
    half = n_head // 2
    span = (half + 1) * rows
    score_scale = HEAD_DIM ** (-0.5)
    exp_scale = score_scale * math.log2(math.e)

    def at_head(off):
        return (c, lax.rem(h + off + n_head, n_head))

    def at_ctx(off):
        return (lax.rem(c + off + n_ctx, n_ctx), h)

    def load(stream, src):
        for j in range(n_head):
            col = pl.multiple_of(lax.rem(h + j, n_head) * HEAD_DIM, HEAD_DIM)
            pltpu.make_async_copy(
                src.at[:, pl.ds(col, HEAD_DIM)], send_in.at[stream, j], load_sem.at[stream]
            ).start()

    def wait_load(stream):
        pltpu.make_async_copy(send_in.at[stream], send_in.at[stream], load_sem.at[stream]).wait()

    load(K, k_hbm)
    load(V, v_hbm)

    barrier = pltpu.get_barrier_semaphore()
    head_steps = [1 << k for k in range(n_head.bit_length() - 1)]
    ctx_steps = [1 << k for k in range(n_ctx.bit_length() - 1)]
    senders = [at_head(d) for d in [-1] + head_steps] + [at_ctx(d) for d in [-1] + ctx_steps]
    for device in senders:
        pl.semaphore_signal(barrier, inc=1, device_id=device, device_id_type=MESH)
    load(Q, q_hbm)
    load(G, g_hbm)
    dk_acc[...] = jnp.zeros_like(dk_acc)
    dv_acc[...] = jnp.zeros_like(dv_acc)
    pl.semaphore_wait(barrier, len(senders))

    def reach(stream, way):
        return half if (stream + way) % 2 == 0 else half - 1

    bufs = ((send_in, in_up, in_down), (send_out, out_up, out_down))

    def ring(phase, stream, way, step):
        far = reach(stream, way)
        count = far - step + 1
        send, up, down = bufs[phase]
        if way == UP:
            store, first = up, step - 1
            src = send.at[stream, pl.ds(1, far)] if step == 1 else up.at[stream, step - 2, pl.ds(first, count)]
        else:
            store, first = down, half - far
            src = (
                send.at[stream, pl.ds(n_head - far, far)]
                if step == 1
                else down.at[stream, step - 2, pl.ds(first, count)]
            )
        return pltpu.make_async_remote_copy(
            src_ref=src,
            dst_ref=store.at[stream, step - 1, pl.ds(first, count)],
            send_sem=ring_ssem.at[phase, way, stream, step - 1],
            recv_sem=ring_rsem.at[phase, way, stream, step - 1],
            device_id=at_head(1 if way == UP else -1),
            device_id_type=MESH,
        )

    def ring_start(phase, stream):
        for way in (UP, DOWN):
            ring(phase, stream, way, 1).start()

    def ring_step(phase, stream, step):
        for way in (UP, DOWN):
            if step <= reach(stream, way):
                ring(phase, stream, way, step).wait_recv()
                if step < reach(stream, way):
                    ring(phase, stream, way, step + 1).start()

    def arrived(phase, stream, way, step):
        if way == UP:
            return bufs[phase][1].at[stream, step - 1, step - 1]
        return bufs[phase][2].at[stream, step - 1, half - step]

    def far_way(stream):
        return UP if reach(stream, UP) == half else DOWN

    wait_load(K)
    ring_start(0, K)
    wait_load(V)
    ring_start(0, V)

    lane = lax.broadcasted_iota(jnp.int32, (8, rows), 1)
    row = lax.broadcasted_iota(jnp.int32, (8, rows), 0)
    keep = jnp.broadcast_to((1 - end_ref[...]).astype(F32) * F32(1.0 - 1.0 / all_rows), (8, rows))
    total = jnp.broadcast_to(rew_ref[...].astype(F32) * 0.001, (8, rows))
    for k in range(rows.bit_length() - 1):
        d = 1 << k
        inside = lane < rows - d
        later_keep = jnp.where(inside, pltpu.roll(keep, rows - d, 1), 1.0)
        later_total = jnp.where(inside, pltpu.roll(total, rows - d, 1), 0.0)
        total = total + keep * later_total
        keep = keep * later_keep
    small[0] = jnp.where(row == 0, total, keep)

    def head_copy(k):
        d = head_steps[k]
        return pltpu.make_async_remote_copy(
            src_ref=small.at[pl.ds(0, d)], dst_ref=small.at[pl.ds(d, d)],
            send_sem=small_ssem.at[k], recv_sem=small_rsem.at[k],
            device_id=at_head(-d), device_id_type=MESH,
        )

    n_small = len(head_steps)
    ctx_moves = [1] + ctx_steps

    def ctx_copy(k):
        return pltpu.make_async_remote_copy(
            src_ref=ctx_val.at[k], dst_ref=ctx_got.at[k],
            send_sem=small_ssem.at[n_small + k], recv_sem=small_rsem.at[n_small + k],
            device_id=at_ctx(-ctx_moves[k]), device_id_type=MESH,
        )

    def splat(ref, index, which):
        return jnp.broadcast_to(ref[index, which : which + 1, 0:1], (1, rows))

    def pair(total_row, keep_row):
        return jnp.where(row == 0, total_row, keep_row)

    def head_move(k):
        head_copy(k).wait_recv()
        if k + 1 < n_small:
            head_copy(k + 1).start()
            return
        after_total, after_keep = jnp.zeros((1, rows), F32), jnp.ones((1, rows), F32)
        for z in reversed(range(n_head)):
            suffix[z] = pair(after_total, after_keep)
            slot = lax.rem(z - h + n_head, n_head)
            z_total, z_keep = splat(small, slot, 0), splat(small, slot, 1)
            after_total = z_total + z_keep * after_total
            after_keep = z_keep * after_keep
        ctx_val[0] = pair(after_total, after_keep)
        ctx_copy(0).start()

    def ctx_move(k):
        ctx_copy(k).wait_recv()
        d = ctx_moves[k]
        got = ctx_got[k]
        ahead = c + d + (0 if k == 0 else 1)
        valid = jnp.broadcast_to(ahead, (8, rows)) < n_ctx
        got_total = jnp.where(valid, jnp.broadcast_to(got[0:1], (8, rows)), 0.0)
        got_keep = jnp.where(valid, jnp.broadcast_to(got[1:2], (8, rows)), 1.0)
        if k == 0:
            ctx_val[1] = jnp.where(row == 0, got_total, got_keep)
        else:
            mine = ctx_val[k]
            my_total = jnp.broadcast_to(mine[0:1], (8, rows))
            my_keep = jnp.broadcast_to(mine[1:2], (8, rows))
            ctx_val[k + 1] = jnp.where(row == 0, my_total + my_keep * got_total, my_keep * got_keep)
        if k + 1 < len(ctx_moves):
            ctx_copy(k + 1).start()

    head_copy(0).start()
    moves = [functools.partial(head_move, k) for k in range(n_small)]
    moves += [functools.partial(ctx_move, k) for k in range(len(ctx_moves))]

    def finish(j, k_raw, v_raw):
        z = lax.rem(h + j, n_head)
        carry = ctx_val[len(ctx_moves), 0:1]
        carry_z = suffix[z, 0:1] + suffix[z, 1:2] * carry
        to_go = small[j, 0:1] + small[j, 1:2] * carry_z
        lifted = to_go * (4 * rows * n_head) ** (-0.5)
        column = jnp.broadcast_to(lifted, (rows, rows)).T
        place = pl.ds(pl.multiple_of((half + z) * rows, rows), rows)
        kbuf[place, :] = (k_raw[...].astype(F32) + column * kdir_ref[pl.ds(h, 1), :]).astype(BF16)
        vbuf[place, :] = (v_raw[...].astype(F32) + column * vdir_ref[pl.ds(h, 1), :]).astype(BF16)

    def finish_step(step):
        if step == 0:
            finish(0, send_in.at[K, 0], send_in.at[V, 0])
        elif step < half:
            finish(n_head - step, arrived(0, K, UP, step), arrived(0, V, UP, step))
            finish(step, arrived(0, K, DOWN, step), arrived(0, V, DOWN, step))
        else:
            finish(half, arrived(0, K, far_way(K), half), arrived(0, V, far_way(V), half))

    per_step = (3, 3, 2, 2)
    q_start = half - 3
    for step in range(1, half + 1):
        if moves:
            for move in moves[: per_step[step - 1]]:
                move()
            moves = moves[per_step[step - 1] :]
        ring_step(0, K, step)
        ring_step(0, V, step)
        if step == q_start:
            wait_load(Q)
            ring_start(0, Q)
            wait_load(G)
            ring_start(0, G)
        if step == len(per_step):
            for done in range(step + 1):
                finish_step(done)
        elif step > len(per_step):
            finish_step(step)

    def halo(which):
        buf = (kbuf, vbuf)[which]
        return pltpu.make_async_remote_copy(
            src_ref=buf.at[pl.ds(n_head * rows, half * rows)], dst_ref=buf.at[pl.ds(0, half * rows)],
            send_sem=halo_ssem.at[which], recv_sem=halo_rsem.at[which],
            device_id=at_ctx(1), device_id_type=MESH,
        )

    halo(0).start()
    halo(1).start()
    q_in[0] = send_in[Q, 0]
    g_in[0] = send_in[G, 0]
    halo(0).wait_recv()
    halo(1).wait_recv()

    def take(step):
        ring_step(0, Q, step)
        ring_step(0, G, step)
        up, down = (UP, DOWN) if step < half else (far_way(Q), far_way(G))
        if step < half:
            q_in[2 * step - 1] = arrived(0, Q, UP, step)[...]
            g_in[2 * step - 1] = arrived(0, G, UP, step)[...]
            q_in[2 * step] = arrived(0, Q, DOWN, step)[...]
            g_in[2 * step] = arrived(0, G, DOWN, step)[...]
        else:
            q_in[2 * step - 1] = arrived(0, Q, up, step)[...]
            g_in[2 * step - 1] = arrived(0, G, down, step)[...]

    def tile(it, carry):
        for step in range(1, half + 1):
            pl.when(it == 2 * step - 1)(functools.partial(take, step))
        odd = lax.rem(it, 2)
        j = odd * (n_head - (it + 1) // 2) + (1 - odd) * (it // 2)
        t = lax.rem(h + j, n_head)
        place = pl.ds(pl.multiple_of(t * rows, rows), span)
        q, g, k, v = q_in[it], g_in[it], kbuf[place, :], vbuf[place, :]
        key = lax.broadcasted_iota(jnp.int32, (span, rows), 0)
        query = lax.broadcasted_iota(jnp.int32, (span, rows), 1)
        before = jnp.where(c == 0, half * rows - t * rows, 0)
        allowed = (key >= jnp.maximum(query + 1, before)) & (key <= query + half * rows)
        s = jnp.where(allowed, dot_nt(k, q), -1e30)
        top = jnp.max(s, axis=0, keepdims=True)
        e = jnp.exp2((s - top) * exp_scale)
        probs = e * (1.0 / jnp.sum(e, axis=0, keepdims=True))
        weights = probs.astype(BF16)
        attended = dot_tn(weights, v).astype(BF16)
        row_dot = jnp.sum((attended.astype(F32) * g.astype(F32)).T, axis=0, keepdims=True)
        slopes = (probs * (dot_nt(v, g) - row_dot) * score_scale).astype(BF16)
        send_out[O, j] = attended
        send_out[DQ, j] = dot_tn(slopes, k).astype(BF16)
        dk_acc[place, :] += jnp.dot(slopes, q, preferred_element_type=F32)
        dv_acc[place, :] += jnp.dot(weights, g, preferred_element_type=F32)
        return carry

    lax.fori_loop(0, n_head, tile, 0)

    ring_start(1, O)
    ring_start(1, DQ)

    grad_send[0] = dk_acc[pl.ds(0, half * rows), :].astype(BF16)
    grad_send[1] = dv_acc[pl.ds(0, half * rows), :].astype(BF16)

    def grad(which):
        return pltpu.make_async_remote_copy(
            src_ref=grad_send.at[which], dst_ref=grad_recv.at[which],
            send_sem=halo_ssem.at[2 + which], recv_sem=halo_rsem.at[2 + which],
            device_id=at_ctx(-1), device_id_type=MESH,
        )

    grad(0).start()
    grad(1).start()
    for z in range(n_head):
        j = lax.rem(z - h + n_head, n_head)
        if z == half:
            grad(0).wait_recv()
            grad(1).wait_recv()
        dk = dk_acc[pl.ds((half + z) * rows, rows), :]
        dv = dv_acc[pl.ds((half + z) * rows, rows), :]
        if z >= half:
            dk = dk + grad_recv[0, pl.ds((z - half) * rows, rows), :].astype(F32)
            dv = dv + grad_recv[1, pl.ds((z - half) * rows, rows), :].astype(F32)
        send_out[DK, j] = dk.astype(BF16)
        send_out[DV, j] = dv.astype(BF16)
    ring_start(1, DK)
    ring_start(1, DV)

    outs = (o_hbm, dq_hbm, dk_hbm, dv_hbm)

    def store(stream, j, src):
        col = pl.multiple_of(lax.rem(h + j, n_head) * HEAD_DIM, HEAD_DIM)
        pltpu.make_async_copy(
            src, outs[stream].at[:, pl.ds(col, HEAD_DIM)], store_sem.at[stream, j]
        ).start()

    for stream in range(4):
        store(stream, 0, send_out.at[stream, 0])
    for step in range(1, half + 1):
        for stream in range(4):
            ring_step(1, stream, step)
            if step < half:
                store(stream, n_head - step, arrived(1, stream, UP, step))
                store(stream, step, arrived(1, stream, DOWN, step))
            else:
                store(stream, half, arrived(1, stream, far_way(stream), half))

    for phase in range(2):
        for stream in range(4):
            for way in (UP, DOWN):
                for step in range(1, reach(stream, way) + 1):
                    ring(phase, stream, way, step).wait_send()
    for k in range(n_small):
        head_copy(k).wait_send()
    for k in range(len(ctx_moves)):
        ctx_copy(k).wait_send()
    for which in range(2):
        halo(which).wait_send()
        grad(which).wait_send()
    for stream in range(4):
        for j in range(n_head):
            pltpu.make_async_copy(
                send_out.at[stream, 0], outs[stream].at[:, pl.ds(0, HEAD_DIM)], store_sem.at[stream, j]
            ).wait()


def on_device(queries, keys_base, values_base, grad_out, key_dir, value_dir, rewards, episode_end):
    rows, features = queries.shape
    n_ctx, n_head = lax.axis_size("ctx"), lax.axis_size("head")
    half = n_head // 2
    all_rows = rows * n_ctx * n_head
    unit = (rows, HEAD_DIM)
    n_small = (n_head.bit_length() - 1) + n_ctx.bit_length()
    ctx_moves = n_ctx.bit_length()
    hbm = pl.BlockSpec(memory_space=pl.ANY)
    vmem = pl.BlockSpec(memory_space=pltpu.VMEM)
    dma = pltpu.SemaphoreType.DMA
    return pl.pallas_call(
        functools.partial(layer, n_ctx, n_head, rows, all_rows),
        out_shape=[jax.ShapeDtypeStruct((rows, features), BF16)] * 4,
        in_specs=[hbm] * 4 + [vmem] * 4,
        out_specs=[hbm] * 4,
        scratch_shapes=[
            pltpu.VMEM((4, n_head) + unit, BF16),
            pltpu.VMEM((4, half, half) + unit, BF16),
            pltpu.VMEM((4, half, half) + unit, BF16),
            pltpu.VMEM((4, n_head) + unit, BF16),
            pltpu.VMEM((4, half, half) + unit, BF16),
            pltpu.VMEM((4, half, half) + unit, BF16),
            pltpu.VMEM(((n_head + half) * rows, HEAD_DIM), BF16),
            pltpu.VMEM(((n_head + half) * rows, HEAD_DIM), BF16),
            pltpu.VMEM(((n_head + half) * rows, HEAD_DIM), F32),
            pltpu.VMEM(((n_head + half) * rows, HEAD_DIM), F32),
            pltpu.VMEM((n_head,) + unit, BF16),
            pltpu.VMEM((n_head,) + unit, BF16),
            pltpu.VMEM((2, half * rows, HEAD_DIM), BF16),
            pltpu.VMEM((2, half * rows, HEAD_DIM), BF16),
            pltpu.VMEM((n_head, 8, rows), F32),
            pltpu.VMEM((n_head, 8, rows), F32),
            pltpu.VMEM((ctx_moves + 1, 8, rows), F32),
            pltpu.VMEM((ctx_moves, 8, rows), F32),
            dma((4,)),
            dma((4, n_head)),
            dma((2, 2, 4, half)),
            dma((2, 2, 4, half)),
            dma((4,)),
            dma((4,)),
            dma((n_small,)),
            dma((n_small,)),
        ],
        compiler_params=pltpu.CompilerParams(
            collective_id=0, has_side_effects=True, vmem_limit_bytes=56 * 2**20
        ),
    )(
        queries, keys_base, values_base, grad_out,
        key_dir.reshape(n_head, HEAD_DIM), value_dir.reshape(n_head, HEAD_DIM),
        rewards.reshape(1, rows), episode_end.reshape(1, rows),
    )


def solution(mesh):
    wide = P(("ctx", "head"), None)
    steps = P(("ctx", "head"))
    return jax.shard_map(
        on_device,
        mesh=mesh,
        in_specs=(wide, wide, wide, wide, P(), P(), steps, steps),
        out_specs=(wide, wide, wide, wide),
        check_vma=False,
    )
```

profile of v0, /device:TPU:1, one launch (start us, length us, event | category | flops | bytes accessed | tf_op | source)
XLA Modules:
  0.0 238.5 jit_solution(16685850678457214681)
XLA Ops:
  0.6 232.7 %shard_map.111 = (bf16[128,2048]{1,0:T(8,128)(2,1)}, bf16[128,2048]{1,0:T(8,128)(2,1)}, bf16[128,2048]{1,0:T(8,128)(2,1)}, bf16[128,2048]{1,0:T(8,128)(2,1)}) custom-call(bf16[128,2048]{1,0:T(8,128)(2,1)} %q_hbm.1, bf16[128,2048]{1,0:T(8,128)(2,1)} %k_hbm.1, bf16[128,2048]{1,0:T(8,128)(2,1)} %v_hbm.1, bf16[128,2048]{1,0:T(8,128)(2,1)} %g_hbm.1, ...), custom_call_target="tpu_custom_call" | custom-call | tf_op jit(solution)/shard_map/pallas_call | solution.py:376
  233.3 0.0 copy-start.2
  233.3 1.9 copy.16
  235.3 0.0 copy-done.2
  235.3 0.0 copy-start.1
  235.3 0.8 copy.17
  236.1 0.4 copy-done.1
  236.5 0.0 copy-start
  236.5 0.8 copy.18
  237.3 0.4 copy-done
  237.7 0.8 copy.19
Async XLA Ops:
  233.3 2.0 copy-start.2
  235.3 1.2 copy-start.1
  236.5 1.2 copy-start
where the time goes:
time: 239 us
  Pallas kernels  233 us (97%)
  local copies, waits for them, and re-layouts  5.19 us (2%)
    pallas_call x1, Pallas kernels, on_device(): pl.pallas_call(functools.partial(layer, n_ctx, n_head, rows, all_rows), o...  233 us
    unnamed x10, local copies, waits for them, and re-layouts  5.19 us

commit v1 on v0

v1 whole, which is shorter than its diff:
```python
import functools
import math

import jax
import jax.numpy as jnp
from jax import lax
from jax.experimental import pallas as pl
from jax.experimental.pallas import tpu as pltpu
from jax.sharding import PartitionSpec as P

HEAD_DIM = 128
BF16 = jnp.bfloat16
F32 = jnp.float32
MESH = pl.DeviceIdType.MESH
K, V, Q, G = range(4)
O, DQ, DK, DV = range(4)
LAG = 0


def dot_nt(a, b):
    return lax.dot_general(a, b, (((1,), (1,)), ((), ())), preferred_element_type=F32)


def dot_tn(a, b):
    return lax.dot_general(a, b, (((0,), (0,)), ((), ())), preferred_element_type=F32)


def layer(
    n_ctx, n_head, rows, all_rows,
    q_hbm, k_hbm, v_hbm, g_hbm, kdir_ref, vdir_ref, rew_ref, end_ref,
    o_hbm, dq_hbm, dk_hbm, dv_hbm,
    got, sent, kbuf, vbuf, dk_acc, dv_acc, grad_send, grad_recv, small, suffix, ctx_val, ctx_got,
    own_sem, in_ssem, in_rsem, out_ssem, out_rsem,
    halo_ssem, halo_rsem, small_ssem, small_rsem, ctx_ssem, ctx_rsem,
):
    c = lax.axis_index("ctx")
    h = lax.axis_index("head")
    half = n_head // 2
    span = (half + 1) * rows
    score_scale = HEAD_DIM ** (-0.5)
    exp_scale = score_scale * math.log2(math.e)
    ins = (k_hbm, v_hbm, q_hbm, g_hbm)
    outs = (o_hbm, dq_hbm, dk_hbm, dv_hbm)
    around = [(d, n_head - d)[way] for d in range(1, half) for way in range(2)] + [half]

    def head_at(off):
        return lax.rem(h + off, n_head)

    def at_ctx(off):
        return (lax.rem(c + off + n_ctx, n_ctx), h)

    def columns(off):
        return pl.ds(pl.multiple_of(head_at(off) * HEAD_DIM, HEAD_DIM), HEAD_DIM)

    def own_in(a):
        return pltpu.make_async_copy(ins[a].at[:, columns(0)], got.at[a, 0], own_sem.at[0, a])

    def own_out(a):
        return pltpu.make_async_copy(sent.at[a, 0], outs[a].at[:, columns(0)], own_sem.at[1, a])

    def send_in(a, j):
        return pltpu.make_async_remote_copy(
            src_ref=ins[a].at[:, columns(j)], dst_ref=got.at[a, n_head - j],
            send_sem=in_ssem.at[a, j], recv_sem=in_rsem.at[a, n_head - j],
            device_id=(c, head_at(j)), device_id_type=MESH,
        )

    def receive_in(a, j):
        return pltpu.make_async_remote_copy(
            src_ref=ins[a].at[:, columns(j)], dst_ref=got.at[a, j],
            send_sem=in_ssem.at[a, j], recv_sem=in_rsem.at[a, j],
            device_id=(c, head_at(j)), device_id_type=MESH,
        )

    def send_out(a, j):
        return pltpu.make_async_remote_copy(
            src_ref=sent.at[a, j], dst_ref=outs[a].at[:, columns(0)],
            send_sem=out_ssem.at[a, j], recv_sem=out_rsem.at[a, n_head - j],
            device_id=(c, head_at(j)), device_id_type=MESH,
        )

    def receive_out(a, j):
        return pltpu.make_async_remote_copy(
            src_ref=sent.at[a, j], dst_ref=outs[a].at[:, columns(j)],
            send_sem=out_ssem.at[a, j], recv_sem=out_rsem.at[a, j],
            device_id=(c, head_at(j)), device_id_type=MESH,
        )

    barrier = pltpu.get_barrier_semaphore()
    ctx_steps = [1 << k for k in range(n_ctx.bit_length() - 1)]
    senders = [(c, head_at(j)) for j in around] + [at_ctx(d) for d in [-1] + ctx_steps]
    for device in senders:
        pl.semaphore_signal(barrier, inc=1, device_id=device, device_id_type=MESH)
    for a in range(4):
        own_in(a).start()
    dk_acc[...] = jnp.zeros_like(dk_acc)
    dv_acc[...] = jnp.zeros_like(dv_acc)

    lane = lax.broadcasted_iota(jnp.int32, (8, rows), 1)
    row = lax.broadcasted_iota(jnp.int32, (8, rows), 0)
    keep = jnp.broadcast_to((1 - end_ref[...]).astype(F32) * F32(1.0 - 1.0 / all_rows), (8, rows))
    total = jnp.broadcast_to(rew_ref[...].astype(F32) * 0.001, (8, rows))
    for k in range(rows.bit_length() - 1):
        d = 1 << k
        inside = lane < rows - d
        later_keep = jnp.where(inside, pltpu.roll(keep, rows - d, 1), 1.0)
        later_total = jnp.where(inside, pltpu.roll(total, rows - d, 1), 0.0)
        total = total + keep * later_total
        keep = keep * later_keep
    small[0] = jnp.where(row == 0, total, keep)
    pl.semaphore_wait(barrier, len(senders))

    def send_small(j):
        return pltpu.make_async_remote_copy(
            src_ref=small.at[0], dst_ref=small.at[n_head - j],
            send_sem=small_ssem.at[j], recv_sem=small_rsem.at[n_head - j],
            device_id=(c, head_at(j)), device_id_type=MESH,
        )

    def receive_small(j):
        return pltpu.make_async_remote_copy(
            src_ref=small.at[0], dst_ref=small.at[j],
            send_sem=small_ssem.at[j], recv_sem=small_rsem.at[j],
            device_id=(c, head_at(j)), device_id_type=MESH,
        )

    for j in around:
        send_small(j).start()
    for j in around:
        send_in(K, j).start()
        send_in(V, j).start()

    ctx_moves = [1] + ctx_steps

    def ctx_copy(k):
        return pltpu.make_async_remote_copy(
            src_ref=ctx_val.at[k], dst_ref=ctx_got.at[k],
            send_sem=ctx_ssem.at[k], recv_sem=ctx_rsem.at[k],
            device_id=at_ctx(-ctx_moves[k]), device_id_type=MESH,
        )

    def splat(ref, index, which):
        return jnp.broadcast_to(ref[index, which : which + 1, 0:1], (1, rows))

    def pair(total_row, keep_row):
        return jnp.where(row == 0, total_row, keep_row)

    for j in around:
        receive_small(j).wait_recv()
    after_total, after_keep = jnp.zeros((1, rows), F32), jnp.ones((1, rows), F32)
    for z in reversed(range(n_head)):
        suffix[z] = pair(after_total, after_keep)
        slot = lax.rem(z - h + n_head, n_head)
        z_total, z_keep = splat(small, slot, 0), splat(small, slot, 1)
        after_total = z_total + z_keep * after_total
        after_keep = z_keep * after_keep
    ctx_val[0] = pair(after_total, after_keep)
    ctx_copy(0).start()
    for k, d in enumerate(ctx_moves):
        ctx_copy(k).wait_recv()
        theirs, mine = ctx_got[k], ctx_val[k]
        ahead = c + d + (0 if k == 0 else 1)
        valid = jnp.broadcast_to(ahead, (8, rows)) < n_ctx
        got_total = jnp.where(valid, jnp.broadcast_to(theirs[0:1], (8, rows)), 0.0)
        got_keep = jnp.where(valid, jnp.broadcast_to(theirs[1:2], (8, rows)), 1.0)
        if k > 0:
            my_total = jnp.broadcast_to(mine[0:1], (8, rows))
            my_keep = jnp.broadcast_to(mine[1:2], (8, rows))
            got_total, got_keep = my_total + my_keep * got_total, my_keep * got_keep
        ctx_val[k + 1] = jnp.where(row == 0, got_total, got_keep)
        if k + 1 < len(ctx_moves):
            ctx_copy(k + 1).start()

    def finish(j):
        z = head_at(j)
        carry = ctx_val[len(ctx_moves), 0:1]
        carry_z = suffix[z, 0:1] + suffix[z, 1:2] * carry
        to_go = small[j, 0:1] + small[j, 1:2] * carry_z
        lifted = to_go * (4 * rows * n_head) ** (-0.5)
        column = jnp.broadcast_to(lifted, (rows, rows)).T
        place = pl.ds(pl.multiple_of((half + z) * rows, rows), rows)
        kbuf[place, :] = (got[K, j].astype(F32) + column * kdir_ref[pl.ds(h, 1), :]).astype(BF16)
        vbuf[place, :] = (got[V, j].astype(F32) + column * vdir_ref[pl.ds(h, 1), :]).astype(BF16)

    own_in(K).wait()
    own_in(V).wait()
    finish(0)
    for at, j in enumerate(around):
        receive_in(K, j).wait_recv()
        receive_in(V, j).wait_recv()
        finish(j)
        if at >= LAG:
            send_in(Q, around[at - LAG]).start()
            send_in(G, around[at - LAG]).start()
    for j in around[len(around) - LAG :]:
        send_in(Q, j).start()
        send_in(G, j).start()

    def halo(which):
        buf = (kbuf, vbuf)[which]
        return pltpu.make_async_remote_copy(
            src_ref=buf.at[pl.ds(n_head * rows, half * rows)], dst_ref=buf.at[pl.ds(0, half * rows)],
            send_sem=halo_ssem.at[which], recv_sem=halo_rsem.at[which],
            device_id=at_ctx(1), device_id_type=MESH,
        )

    halo(0).start()
    halo(1).start()
    own_in(Q).wait()
    own_in(G).wait()
    halo(0).wait_recv()
    halo(1).wait_recv()

    def slot_of(it):
        odd = lax.rem(it, 2)
        return odd * (n_head - (it + 1) // 2) + (1 - odd) * (it // 2)

    def tile(it, carry):
        j = slot_of(it)

        @pl.when(it > 0)
        def _():
            receive_in(Q, j).wait_recv()
            receive_in(G, j).wait_recv()

        t = head_at(j)
        place = pl.ds(pl.multiple_of(t * rows, rows), span)
        q, g, k, v = got[Q, j], got[G, j], kbuf[place, :], vbuf[place, :]
        key = lax.broadcasted_iota(jnp.int32, (span, rows), 0)
        query = lax.broadcasted_iota(jnp.int32, (span, rows), 1)
        before = jnp.where(c == 0, half * rows - t * rows, 0)
        allowed = (key >= jnp.maximum(query + 1, before)) & (key <= query + half * rows)
        s = jnp.where(allowed, dot_nt(k, q), -1e30)
        top = jnp.max(s, axis=0, keepdims=True)
        e = jnp.exp2((s - top) * exp_scale)
        probs = e * (1.0 / jnp.sum(e, axis=0, keepdims=True))
        weights = probs.astype(BF16)
        attended = dot_tn(weights, v).astype(BF16)
        row_dot = jnp.sum((attended.astype(F32) * g.astype(F32)).T, axis=0, keepdims=True)
        slopes = (probs * (dot_nt(v, g) - row_dot) * score_scale).astype(BF16)
        sent[O, j] = attended
        sent[DQ, j] = dot_tn(slopes, k).astype(BF16)

        @pl.when(it > 0)
        def _():
            send_out(O, j).start()
            send_out(DQ, j).start()

        dk_acc[place, :] += jnp.dot(slopes, q, preferred_element_type=F32)
        dv_acc[place, :] += jnp.dot(weights, g, preferred_element_type=F32)
        return carry

    lax.fori_loop(0, n_head, tile, 0)

    grad_send[0] = dk_acc[pl.ds(0, half * rows), :].astype(BF16)
    grad_send[1] = dv_acc[pl.ds(0, half * rows), :].astype(BF16)

    def grad(which):
        return pltpu.make_async_remote_copy(
            src_ref=grad_send.at[which], dst_ref=grad_recv.at[which],
            send_sem=halo_ssem.at[2 + which], recv_sem=halo_rsem.at[2 + which],
            device_id=at_ctx(-1), device_id_type=MESH,
        )

    grad(0).start()
    grad(1).start()
    own_out(O).start()
    own_out(DQ).start()
    grad(0).wait_recv()
    grad(1).wait_recv()

    def collect(it, carry):
        j = slot_of(it)
        z = head_at(j)
        place = pl.ds(pl.multiple_of((half + z) * rows, rows), rows)
        back = pl.ds(pl.multiple_of(jnp.maximum(z - half, 0) * rows, rows), rows)
        for which, acc in enumerate((dk_acc, dv_acc)):
            returned = jnp.where(z >= half, grad_recv[which, back, :].astype(F32), 0.0)
            sent[DK + which, j] = (acc[place, :] + returned).astype(BF16)

        @pl.when(it > 0)
        def _():
            send_out(DK, j).start()
            send_out(DV, j).start()

        return carry

    lax.fori_loop(0, n_head, collect, 0)
    own_out(DK).start()
    own_out(DV).start()

    for j in around:
        send_small(j).wait_send()
    for k in range(len(ctx_moves)):
        ctx_copy(k).wait_send()
    for which in range(2):
        halo(which).wait_send()
        grad(which).wait_send()
    for a in range(4):
        own_out(a).wait()
        for j in around:
            send_in(a, j).wait_send()
            send_out(a, j).wait_send()
            receive_out(a, j).wait_recv()


def on_device(queries, keys_base, values_base, grad_out, key_dir, value_dir, rewards, episode_end):
    rows, features = queries.shape
    n_ctx, n_head = lax.axis_size("ctx"), lax.axis_size("head")
    half = n_head // 2
    all_rows = rows * n_ctx * n_head
    unit = (rows, HEAD_DIM)
    ctx_moves = n_ctx.bit_length()
    hbm = pl.BlockSpec(memory_space=pl.ANY)
    vmem = pl.BlockSpec(memory_space=pltpu.VMEM)
    dma = pltpu.SemaphoreType.DMA
    return pl.pallas_call(
        functools.partial(layer, n_ctx, n_head, rows, all_rows),
        out_shape=[jax.ShapeDtypeStruct((rows, features), BF16)] * 4,
        in_specs=[hbm] * 4 + [vmem] * 4,
        out_specs=[hbm] * 4,
        scratch_shapes=[
            pltpu.VMEM((4, n_head) + unit, BF16),
            pltpu.VMEM((4, n_head) + unit, BF16),
            pltpu.VMEM(((n_head + half) * rows, HEAD_DIM), BF16),
            pltpu.VMEM(((n_head + half) * rows, HEAD_DIM), BF16),
            pltpu.VMEM(((n_head + half) * rows, HEAD_DIM), F32),
            pltpu.VMEM(((n_head + half) * rows, HEAD_DIM), F32),
            pltpu.VMEM((2, half * rows, HEAD_DIM), BF16),
            pltpu.VMEM((2, half * rows, HEAD_DIM), BF16),
            pltpu.VMEM((n_head, 8, rows), F32),
            pltpu.VMEM((n_head, 8, rows), F32),
            pltpu.VMEM((ctx_moves + 1, 8, rows), F32),
            pltpu.VMEM((ctx_moves, 8, rows), F32),
            dma((2, 4)),
            dma((4, n_head)),
            dma((4, n_head)),
            dma((4, n_head)),
            dma((4, n_head)),
            dma((4,)),
            dma((4,)),
            dma((n_head,)),
            dma((n_head,)),
            dma((ctx_moves,)),
            dma((ctx_moves,)),
        ],
        compiler_params=pltpu.CompilerParams(
            collective_id=0, has_side_effects=True, vmem_limit_bytes=48 * 2**20
        ),
    )(
        queries, keys_base, values_base, grad_out,
        key_dir.reshape(n_head, HEAD_DIM), value_dir.reshape(n_head, HEAD_DIM),
        rewards.reshape(1, rows), episode_end.reshape(1, rows),
    )


def solution(mesh):
    wide = P(("ctx", "head"), None)
    steps = P(("ctx", "head"))
    return jax.shard_map(
        on_device,
        mesh=mesh,
        in_specs=(wide, wide, wide, wide, P(), P(), steps, steps),
        out_specs=(wide, wide, wide, wide),
        check_vma=False,
    )
```

time: 239 us -> 215 us (0.90)
  Pallas kernels: 233 us -> 203 us
  local copies, waits for them, and re-layouts: 5.19 us -> 9.39 us
    pallas_call x1, Pallas kernels: 233 us -> 203 us  [on_device(): pl.pallas_call(functools.partial(layer, n_ctx, n_head, rows, all_rows), o...]
    unnamed x10 -> x20, local copies, waits for them, and re-layouts: 5.19 us -> 9.39 us
where the time goes in v1:
time: 215 us; the launch traced here: 213 us
  Pallas kernels  203 us (94%)
  local copies, waits for them, and re-layouts  9.39 us (4%)
    pallas_call x1, Pallas kernels, on_device(): pl.pallas_call(functools.partial(layer, n_ctx, n_head, rows, all_rows), o...  203 us
    unnamed x20, local copies, waits for them, and re-layouts  9.39 us

profile of v1, /device:TPU:1, one launch (start us, length us, event | category | flops | bytes accessed | tf_op | source)
XLA Modules:
  0.0 213.2 jit_solution(13438033697859297583)
XLA Ops:
  0.6 0.0 copy-start.6
  0.6 0.0 copy-start.7
  0.7 0.6 copy-done.6
  1.3 0.0 copy-done.7
  1.3 0.0 copy-start
  1.3 1.0 copy-done
  2.3 0.0 copy-start.1
  2.4 1.0 copy-done.1
  3.4 0.0 copy-start.2
  3.4 1.0 copy-done.2
  4.4 0.0 copy-start.3
  4.4 1.0 copy-done.3
  5.5 0.0 copy-start.4
  5.5 0.7 copy-done.4
  6.2 0.0 copy-start.5
  6.2 0.7 copy-done.5
  6.9 203.2 %shard_map.111 = (bf16[128,2048]{1,0:T(8,128)(2,1)S(1)}, bf16[128,2048]{1,0:T(8,128)(2,1)S(1)}, bf16[128,2048]{1,0:T(8,128)(2,1)S(1)}, bf16[128,2048]{1,0:T(8,128)(2,1)S(1)}) custom-call(bf16[128,2048]{1,0:T(8,128)(2,1)S(1)} %copy-done, bf16[128,2048]{1,0:T(8,128)(2,1)S(1)} %copy-done.1, bf16[128,2048]{1,0:T(8,128)(2,1)S(1)} %copy-done.2, ...), custom_call_target="tpu_custom_call" | custom-call | tf_op jit(solution)/shard_map/pallas_call | solution.py:317
  210.1 0.8 copy.16
  210.9 0.8 copy.17
  211.7 0.8 copy.18
  212.5 0.8 copy.19
Async XLA Ops:
  0.6 0.7 copy-start.6
  0.6 0.7 copy-start.7
  1.3 1.0 copy-start
  2.3 1.0 copy-start.1
  3.4 1.0 copy-start.2
  4.4 1.0 copy-start.3
  5.5 0.7 copy-start.4
  6.2 0.7 copy-start.5

commit v2 on v1

--- a/solution.py
+++ b/solution.py
@@ -14,7 +14,7 @@
 MESH = pl.DeviceIdType.MESH
 K, V, Q, G = range(4)
 O, DQ, DK, DV = range(4)
-LAG = 0
+FIRST = 3
 
 
 def dot_nt(a, b):
@@ -27,10 +27,10 @@
 
 def layer(
     n_ctx, n_head, rows, all_rows,
-    q_hbm, k_hbm, v_hbm, g_hbm, kdir_ref, vdir_ref, rew_ref, end_ref,
+    q_hbm, k_hbm, v_hbm, g_hbm, kdir_hbm, vdir_hbm, rew_hbm, end_hbm,
     o_hbm, dq_hbm, dk_hbm, dv_hbm,
-    got, sent, kbuf, vbuf, dk_acc, dv_acc, grad_send, grad_recv, small, suffix, ctx_val, ctx_got,
-    own_sem, in_ssem, in_rsem, out_ssem, out_rsem,
+    kdir_ref, vdir_ref, rew_ref, end_ref, got, sent, kbuf, vbuf, dk_acc, dv_acc, grad_send, grad_recv, small, suffix, ctx_val, ctx_got,
+    vec_sem, own_sem, in_ssem, in_rsem, out_ssem, out_rsem,
     halo_ssem, halo_rsem, small_ssem, small_rsem, ctx_ssem, ctx_rsem,
 ):
     c = lax.axis_index("ctx")
@@ -41,7 +41,7 @@
     exp_scale = score_scale * math.log2(math.e)
     ins = (k_hbm, v_hbm, q_hbm, g_hbm)
     outs = (o_hbm, dq_hbm, dk_hbm, dv_hbm)
-    around = [(d, n_head - d)[way] for d in range(1, half) for way in range(2)] + [half]
+    around = [half] + [(d, n_head - d)[way] for d in reversed(range(1, half)) for way in range(2)]
 
     def head_at(off):
         return lax.rem(h + off, n_head)
@@ -91,11 +91,21 @@
     senders = [(c, head_at(j)) for j in around] + [at_ctx(d) for d in [-1] + ctx_steps]
     for device in senders:
         pl.semaphore_signal(barrier, inc=1, device_id=device, device_id_type=MESH)
-    for a in range(4):
-        own_in(a).start()
-    dk_acc[...] = jnp.zeros_like(dk_acc)
-    dv_acc[...] = jnp.zeros_like(dv_acc)
-
+    vectors = [
+        pltpu.make_async_copy(src, dst, vec_sem.at[i])
+        for i, (src, dst) in enumerate(
+            ((rew_hbm, rew_ref), (end_hbm, end_ref), (kdir_hbm, kdir_ref), (vdir_hbm, vdir_ref))
+        )
+    ]
+    for copy in vectors:
+        copy.start()
+    pl.semaphore_wait(barrier, len(senders))
+    for j in around[:FIRST]:
+        send_in(K, j).start()
+        send_in(V, j).start()
+
+    vectors[0].wait()
+    vectors[1].wait()
     lane = lax.broadcasted_iota(jnp.int32, (8, rows), 1)
     row = lax.broadcasted_iota(jnp.int32, (8, rows), 0)
     keep = jnp.broadcast_to((1 - end_ref[...]).astype(F32) * F32(1.0 - 1.0 / all_rows), (8, rows))
@@ -108,8 +118,6 @@
         total = total + keep * later_total
         keep = keep * later_keep
     small[0] = jnp.where(row == 0, total, keep)
-    pl.semaphore_wait(barrier, len(senders))
-
     def send_small(j):
         return pltpu.make_async_remote_copy(
             src_ref=small.at[0], dst_ref=small.at[n_head - j],
@@ -126,9 +134,13 @@
 
     for j in around:
         send_small(j).start()
-    for j in around:
+    for j in around[FIRST:]:
         send_in(K, j).start()
         send_in(V, j).start()
+    for a in range(4):
+        own_in(a).start()
+    dk_acc[...] = jnp.zeros_like(dk_acc)
+    dv_acc[...] = jnp.zeros_like(dv_acc)
 
     ctx_moves = [1] + ctx_steps
 
@@ -182,19 +194,17 @@
         kbuf[place, :] = (got[K, j].astype(F32) + column * kdir_ref[pl.ds(h, 1), :]).astype(BF16)
         vbuf[place, :] = (got[V, j].astype(F32) + column * vdir_ref[pl.ds(h, 1), :]).astype(BF16)
 
+    vectors[2].wait()
+    vectors[3].wait()
     own_in(K).wait()
     own_in(V).wait()
     finish(0)
-    for at, j in enumerate(around):
+    for j in around:
         receive_in(K, j).wait_recv()
         receive_in(V, j).wait_recv()
-        finish(j)
-        if at >= LAG:
-            send_in(Q, around[at - LAG]).start()
-            send_in(G, around[at - LAG]).start()
-    for j in around[len(around) - LAG :]:
         send_in(Q, j).start()
         send_in(G, j).start()
+        finish(j)
 
     def halo(which):
         buf = (kbuf, vbuf)[which]
@@ -212,13 +222,14 @@
     halo(1).wait_recv()
 
     def slot_of(it):
+        far = half - (it + 1) // 2
         odd = lax.rem(it, 2)
-        return odd * (n_head - (it + 1) // 2) + (1 - odd) * (it // 2)
+        return odd * far + (1 - odd) * (n_head - far)
 
     def tile(it, carry):
         j = slot_of(it)
 
-        @pl.when(it > 0)
+        @pl.when(it < n_head - 1)
         def _():
             receive_in(Q, j).wait_recv()
             receive_in(G, j).wait_recv()
@@ -241,7 +252,7 @@
         sent[O, j] = attended
         sent[DQ, j] = dot_tn(slopes, k).astype(BF16)
 
-        @pl.when(it > 0)
+        @pl.when(it < n_head - 1)
         def _():
             send_out(O, j).start()
             send_out(DQ, j).start()
@@ -278,7 +289,7 @@
             returned = jnp.where(z >= half, grad_recv[which, back, :].astype(F32), 0.0)
             sent[DK + which, j] = (acc[place, :] + returned).astype(BF16)
 
-        @pl.when(it > 0)
+        @pl.when(it < n_head - 1)
         def _():
             send_out(DK, j).start()
             send_out(DV, j).start()
@@ -312,14 +323,17 @@
     unit = (rows, HEAD_DIM)
     ctx_moves = n_ctx.bit_length()
     hbm = pl.BlockSpec(memory_space=pl.ANY)
-    vmem = pl.BlockSpec(memory_space=pltpu.VMEM)
     dma = pltpu.SemaphoreType.DMA
     return pl.pallas_call(
         functools.partial(layer, n_ctx, n_head, rows, all_rows),
         out_shape=[jax.ShapeDtypeStruct((rows, features), BF16)] * 4,
-        in_specs=[hbm] * 4 + [vmem] * 4,
+        in_specs=[hbm] * 8,
         out_specs=[hbm] * 4,
         scratch_shapes=[
+            pltpu.VMEM((n_head, HEAD_DIM), F32),
+            pltpu.VMEM((n_head, HEAD_DIM), F32),
+            pltpu.VMEM((1, rows), jnp.int32),
+            pltpu.VMEM((1, rows), jnp.int32),
             pltpu.VMEM((4, n_head) + unit, BF16),
             pltpu.VMEM((4, n_head) + unit, BF16),
             pltpu.VMEM(((n_head + half) * rows, HEAD_DIM), BF16),
@@ -332,6 +346,7 @@
             pltpu.VMEM((n_head, 8, rows), F32),
             pltpu.VMEM((ctx_moves + 1, 8, rows), F32),
             pltpu.VMEM((ctx_moves, 8, rows), F32),
+            dma((4,)),
             dma((2, 4)),
             dma((4, n_head)),
             dma((4, n_head)),
@@ -345,7 +360,7 @@
             dma((ctx_moves,)),
         ],
         compiler_params=pltpu.CompilerParams(
-            collective_id=0, has_side_effects=True, vmem_limit_bytes=48 * 2**20
+            collective_id=0, has_side_effects=True, vmem_limit_bytes=60 * 2**20
         ),
     )(
         queries, keys_base, values_base, grad_out,

time: 215 us -> 209 us (0.972)
  local copies, waits for them, and re-layouts: 9.39 us -> 5.19 us
    unnamed x20 -> x10, local copies, waits for them, and re-layouts: 9.39 us -> 5.19 us
where the time goes in v2:
time: 209 us; the launch traced here: 208 us
  Pallas kernels  203 us (97%)
  local copies, waits for them, and re-layouts  5.19 us (2%)
    pallas_call x1, Pallas kernels, on_device(): pl.pallas_call(functools.partial(layer, n_ctx, n_head, rows, all_rows), o...  203 us
    unnamed x10, local copies, waits for them, and re-layouts  5.19 us

profile of v2, /device:TPU:1, one launch (start us, length us, event | category | flops | bytes accessed | tf_op | source)
XLA Modules:
  0.0 208.5 jit_solution(12963528132592651006)
XLA Ops:
  0.6 202.6 %shard_map.111 = (bf16[128,2048]{1,0:T(8,128)(2,1)}, bf16[128,2048]{1,0:T(8,128)(2,1)}, bf16[128,2048]{1,0:T(8,128)(2,1)}, bf16[128,2048]{1,0:T(8,128)(2,1)}) custom-call(bf16[128,2048]{1,0:T(8,128)(2,1)} %q_hbm.1, bf16[128,2048]{1,0:T(8,128)(2,1)} %k_hbm.1, bf16[128,2048]{1,0:T(8,128)(2,1)} %v_hbm.1, bf16[128,2048]{1,0:T(8,128)(2,1)} %g_hbm.1, ...), custom_call_target="tpu_custom_call" | custom-call | tf_op jit(solution)/shard_map/pallas_call | solution.py:327
  203.3 0.0 copy-start.2
  203.3 1.9 copy.16
  205.2 0.0 copy-done.2
  205.2 0.0 copy-start.1
  205.2 0.8 copy.17
  206.0 0.4 copy-done.1
  206.5 0.0 copy-start
  206.5 0.8 copy.18
  207.3 0.4 copy-done
  207.7 0.8 copy.19
Async XLA Ops:
  203.3 2.0 copy-start.2
  205.2 1.2 copy-start.1
  206.5 1.2 copy-start

commit v3 on v2

--- a/solution.py
+++ b/solution.py
@@ -15,6 +15,7 @@
 K, V, Q, G = range(4)
 O, DQ, DK, DV = range(4)
 FIRST = 3
+PIECES = 2
 
 
 def dot_nt(a, b):
@@ -315,6 +316,26 @@
             receive_out(a, j).wait_recv()
 
 
+def hand_over(*refs):
+    held, in_sem, out_sem = refs[8:]
+    rows = refs[0].shape[0] // PIECES
+    pieces = [(a, i, pl.ds(i * rows, rows)) for a in range(4) for i in range(PIECES)]
+
+    def inward(a, i, part):
+        return pltpu.make_async_copy(refs[a].at[part], held.at[a, part], in_sem.at[a, i])
+
+    def outward(a, i, part):
+        return pltpu.make_async_copy(held.at[a, part], refs[4 + a].at[part], out_sem.at[a, i])
+
+    for piece in pieces:
+        inward(*piece).start()
+    for piece in pieces:
+        inward(*piece).wait()
+        outward(*piece).start()
+    for piece in pieces:
+        outward(*piece).wait()
+
+
 def on_device(queries, keys_base, values_base, grad_out, key_dir, value_dir, rewards, episode_end):
     rows, features = queries.shape
     n_ctx, n_head = lax.axis_size("ctx"), lax.axis_size("head")
@@ -324,7 +345,7 @@
     ctx_moves = n_ctx.bit_length()
     hbm = pl.BlockSpec(memory_space=pl.ANY)
     dma = pltpu.SemaphoreType.DMA
-    return pl.pallas_call(
+    results = pl.pallas_call(
         functools.partial(layer, n_ctx, n_head, rows, all_rows),
         out_shape=[jax.ShapeDtypeStruct((rows, features), BF16)] * 4,
         in_specs=[hbm] * 8,
@@ -367,6 +388,14 @@
         key_dir.reshape(n_head, HEAD_DIM), value_dir.reshape(n_head, HEAD_DIM),
         rewards.reshape(1, rows), episode_end.reshape(1, rows),
     )
+    return pl.pallas_call(
+        hand_over,
+        out_shape=[jax.ShapeDtypeStruct((rows, features), BF16)] * 4,
+        in_specs=[hbm] * 4,
+        out_specs=[hbm] * 4,
+        scratch_shapes=[pltpu.VMEM((4, rows, features), BF16), dma((4, PIECES)), dma((4, PIECES))],
+        compiler_params=pltpu.CompilerParams(vmem_limit_bytes=60 * 2**20),
+    )(*results)
 
 
 def solution(mesh):

time: 209 us -> 206 us (0.986)
  local copies, waits for them, and re-layouts: 5.19 us -> 0 us
    unnamed x10 -> x0, local copies, waits for them, and re-layouts: 5.19 us -> none
    pallas_call x0 -> x1, Pallas kernels: none -> 2.4 us  [on_device(): pl.pallas_call(hand_over, out_shape=[jax.ShapeDtypeStruct((rows, features...]
where the time goes in v3:
time: 206 us
  Pallas kernels  205 us (100%)
    pallas_call x1, Pallas kernels, on_device(): pl.pallas_call(functools.partial(layer, n_ctx, n_head, rows, all_rows), o...  203 us

profile of v3, /device:TPU:1, one launch (start us, length us, event | category | flops | bytes accessed | tf_op | source)
XLA Modules:
  0.0 205.7 jit_solution(6992306376383499124)
XLA Ops:
  0.6 202.6 %shard_map.111 = (bf16[128,2048]{1,0:T(8,128)(2,1)}, bf16[128,2048]{1,0:T(8,128)(2,1)}, bf16[128,2048]{1,0:T(8,128)(2,1)}, bf16[128,2048]{1,0:T(8,128)(2,1)}) custom-call(bf16[128,2048]{1,0:T(8,128)(2,1)} %q_hbm.1, bf16[128,2048]{1,0:T(8,128)(2,1)} %k_hbm.1, bf16[128,2048]{1,0:T(8,128)(2,1)} %v_hbm.1, bf16[128,2048]{1,0:T(8,128)(2,1)} %g_hbm.1, ...), custom_call_target="tpu_custom_call" | custom-call | tf_op jit(solution)/shard_map/pallas_call | solution.py:348
  203.3 2.4 %shard_map.112 = (bf16[128,2048]{1,0:T(8,128)(2,1)}, bf16[128,2048]{1,0:T(8,128)(2,1)}, bf16[128,2048]{1,0:T(8,128)(2,1)}, bf16[128,2048]{1,0:T(8,128)(2,1)}) custom-call(bf16[128,2048]{1,0:T(8,128)(2,1)} %get-tuple-element.8.refs_0_, bf16[128,2048]{1,0:T(8,128)(2,1)} %get-tuple-element.9.refs_1_, bf16[128,2048]{1,0:T(8,128)(2,1)} %get-tuple-element.10.refs_2_, ...), custom_call_target="tpu_custom_call" | custom-call | tf_op jit(solution)/shard_map/pallas_call | solution.py:391

commit v4 on v3

--- a/solution.py
+++ b/solution.py
@@ -118,7 +118,7 @@
         later_total = jnp.where(inside, pltpu.roll(total, rows - d, 1), 0.0)
         total = total + keep * later_total
         keep = keep * later_keep
-    small[0] = jnp.where(row == 0, total, keep)
+    small[0] = jnp.where(row == 0, total, keep)[0:2]
     def send_small(j):
         return pltpu.make_async_remote_copy(
             src_ref=small.at[0], dst_ref=small.at[n_head - j],
@@ -363,7 +363,7 @@
             pltpu.VMEM(((n_head + half) * rows, HEAD_DIM), F32),
             pltpu.VMEM((2, half * rows, HEAD_DIM), BF16),
             pltpu.VMEM((2, half * rows, HEAD_DIM), BF16),
-            pltpu.VMEM((n_head, 8, rows), F32),
+            pltpu.VMEM((n_head, 2, rows), F32),
             pltpu.VMEM((n_head, 8, rows), F32),
             pltpu.VMEM((ctx_moves + 1, 8, rows), F32),
             pltpu.VMEM((ctx_moves, 8, rows), F32),

time: 206 us -> 204 us (level)
    pallas_call x1, Pallas kernels: 203 us -> 201 us  [on_device(): pl.pallas_call(functools.partial(layer, n_ctx, n_head, rows, all_rows), o...]
where the time goes in v4:
time: 204 us
  Pallas kernels  203 us (100%)
    pallas_call x1, Pallas kernels, on_device(): pl.pallas_call(functools.partial(layer, n_ctx, n_head, rows, all_rows), o...  201 us

profile of v4, /device:TPU:1, one launch (start us, length us, event | category | flops | bytes accessed | tf_op | source)
XLA Modules:
  0.0 203.6 jit_solution(6070100952644244900)
XLA Ops:
  0.6 200.5 %shard_map.111 = (bf16[128,2048]{1,0:T(8,128)(2,1)}, bf16[128,2048]{1,0:T(8,128)(2,1)}, bf16[128,2048]{1,0:T(8,128)(2,1)}, bf16[128,2048]{1,0:T(8,128)(2,1)}) custom-call(bf16[128,2048]{1,0:T(8,128)(2,1)} %q_hbm.1, bf16[128,2048]{1,0:T(8,128)(2,1)} %k_hbm.1, bf16[128,2048]{1,0:T(8,128)(2,1)} %v_hbm.1, bf16[128,2048]{1,0:T(8,128)(2,1)} %g_hbm.1, ...), custom_call_target="tpu_custom_call" | custom-call | tf_op jit(solution)/shard_map/pallas_call | solution.py:348
  201.2 2.4 %shard_map.112 = (bf16[128,2048]{1,0:T(8,128)(2,1)}, bf16[128,2048]{1,0:T(8,128)(2,1)}, bf16[128,2048]{1,0:T(8,128)(2,1)}, bf16[128,2048]{1,0:T(8,128)(2,1)}) custom-call(bf16[128,2048]{1,0:T(8,128)(2,1)} %get-tuple-element.8.refs_0_, bf16[128,2048]{1,0:T(8,128)(2,1)} %get-tuple-element.9.refs_1_, bf16[128,2048]{1,0:T(8,128)(2,1)} %get-tuple-element.10.refs_2_, ...), custom_call_target="tpu_custom_call" | custom-call | tf_op jit(solution)/shard_map/pallas_call | solution.py:391
